TPU v7x, 32 devices: a whole 2x2x4 slice. The times are simulated.
32 devices in a mesh: out: 4 (over z), con: 4 (over y, core), occ: 2 (over x).
Axes of the slice: x: 2, y: 2, z: 4, core: 2. Of those that a mesh axis runs over, the one named last changes fastest.
Arguments:
- amplitudes: float32 [512, 64, 64], P('con', 'occ', 'out'), may hold values from -6 to 6
- fit_out: float32 [1024, 256], P('con', 'out'), may hold values from -0.12 to 0.12
- fit_con: float32 [1024, 512], P(None, 'con'), may hold values from -0.12 to 0.12
- hole_hole: float32 [64, 64], replicated, may hold values from -0.75 to 0.75
Outputs:
- ladder: float32 [256, 64, 64], P(('out', 'con'), 'occ')
All inputs are finite; a program needn't handle non-finite values.
Results may differ from a plain program's by a relative error of at most 0.000075.
Values sent between devices are 32-bit elements; how exact they have to be, the bound alone decides.
A program may use at most 64 MiB of HBM per device.

v0:
```python
import jax
import jax.numpy as jnp
from jax import lax
from jax.sharding import PartitionSpec as P

highest = lax.Precision.HIGHEST


def local(amplitudes, fit_out, fit_con, hole_hole):
    norbs = hole_hole.shape[0]
    dress = jnp.eye(norbs, dtype=jnp.float32) - hole_hole
    tile = jnp.dot(lax.all_gather(fit_out, "con", axis=0, tiled=True).T, fit_con, precision=highest)
    whole = lax.all_gather(amplitudes, "out", axis=2, tiled=True)
    kept_rows = tile.shape[0] // lax.axis_size("con")
    flat = whole.reshape(whole.shape[0], -1)
    product = jnp.dot(tile, flat, precision=highest)
    summed = lax.psum_scatter(
        product.reshape(lax.axis_size("con") * kept_rows, whole.shape[1], whole.shape[2]),
        "con",
        scatter_dimension=0,
        tiled=True,
    )
    right = jnp.einsum("qim,jm->qij", summed, dress, precision=highest)
    complete = lax.all_gather(right, "occ", axis=1, tiled=True)
    own = summed.shape[1]
    first = lax.axis_index("occ") * own
    rows_dress = lax.dynamic_slice_in_dim(dress, first, own, 0)
    ladder = jnp.einsum("im,pmj->pij", rows_dress, complete, precision=highest)
    return ladder


def solution(mesh):
    placed = (P("con", "occ", "out"), P("con", "out"), P(None, "con"), P())
    return jax.shard_map(
        local, mesh=mesh, in_specs=placed, out_specs=P(("out", "con"), "occ", None), check_vma=False
    )
```

profile of v0, /device:TPU:0, one launch (start us, length us, event | category | flops | bytes accessed | tf_op | source)
XLA Modules:
  0.0 88.1 jit_solution(10908262456737044939)
XLA Ops:
  6.5 0.0 copy-start
  6.5 0.0 copy-start.2
  6.5 0.0 all-gather.2.cloned.1.call-start
  6.5 0.7 all-gather.2.cloned.1.call-update
  7.3 0.0 reduce-scatter.2.cloned.1.call-start
  7.3 0.1 copy-done.2
  7.4 7.2 %all_gather.9 = f32[1024,64]{0,1:T(8,128)S(1)} all-gather(f32[256,64]{0,1:T(8,128)S(1)} %copy-done.2), channel_id=1, replica_groups=mesh['out'=4,'con'=4,'occ'=2] {'con'}, dimensions={0}, use_global_device_ids=true | all-gather | bytes 327680 | tf_op jit(solution)/shard_map/all_gather | solution.py:12
  14.6 0.0 copy-done
  14.6 0.4 convolution_bitcast_fusion.1
  15.1 24.5 %all-gather.2.cloned.1.call-done = f32[128,32,64]{0,2,1:T(8,128)} async-done(((f32[128,32,16]{0,2,1:T(8,128)}), f32[128,32,64]{0,2,1:T(8,128)}) %all-gather.2.cloned.1.call-update) | async-done | bytes 1048592 | tf_op jit(solution)/shard_map/all_gather | solution.py:13
  39.6 4.3 %fusion = f32[64,32,64]{2,0,1:T(8,128)S(1)} fusion(f32[64,128,1]{1,0,2:T(8,128)S(1)} %convolution_bitcast_fusion.1, f32[128,32,64]{0,2,1:T(8,128)} %all-gather.2.cloned.1.call-done), kind=kOutput, calls=%fused_computation.2 | convolution fusion | flops 201326592 | bytes 1605632 | tf_op jit(solution)/shard_map/dot_general | solution.py:16
  43.9 1.6 %copy.5 = f32[64,32,64]{2,1,0:T(8,128)} copy(f32[64,32,64]{2,0,1:T(8,128)S(1)} %fusion) | data formatting | bytes 1048576 | tf_op jit(solution)/shard_map/dot_general | solution.py:16
  45.5 0.0 copy-start.1
  45.5 0.0 reduce-scatter.2.cloned.1.call-update
  45.5 0.7 copy-done.1
  46.3 23.8 %reduce-scatter.2.cloned.1.call-done = f32[16,32,64]{2,1,0:T(8,128)} async-done(((f32[64,32,64]{2,1,0:T(8,128)}), f32[16,32,64]{2,1,0:T(8,128)}) %reduce-scatter.2.cloned.1.call-update) | async-done | bytes 131088 | tf_op jit(solution)/shard_map/reduce_scatter | solution.py:17
  70.1 1.3 %fusion.2 = f32[16,32,64]{2,1,0:T(8,128)S(1)} fusion(f32[16,32,64]{2,1,0:T(8,128)} %reduce-scatter.2.cloned.1.call-done, f32[64,64]{1,0:T(8,128)S(1)} %copy-done.1), kind=kOutput, calls=%fused_computation.4 | convolution fusion | flops 25178112 | bytes 278528 | tf_op jit(solution)/shard_map/qim,jm->qij/dot_general | solution.py:23
  71.4 8.7 %all_gather.11 = f32[16,64,64]{2,1,0:T(8,128)S(1)} all-gather(f32[16,32,64]{2,1,0:T(8,128)S(1)} %fusion.2), channel_id=1, replica_groups=mesh['out'=4,'con'=4,'occ'=2] {'occ'}, dimensions={1}, use_global_device_ids=true | all-gather | bytes 393216 | tf_op jit(solution)/shard_map/all_gather | solution.py:24
  80.1 1.1 %convolution_bitcast_fusion = f32[16,32,64]{2,1,0:T(8,128)} fusion(f32[16,64,64]{2,1,0:T(8,128)S(1)} %all_gather.11, f32[64,64]{1,0:T(8,128)S(1)} %convert_subtract_fusion, s32[]{:T(128)S(6)} %select_n.3), kind=kOutput, calls=%fused_computation | convolution fusion | flops 25165824 | bytes 671748 | tf_op jit(solution)/shard_map/im,pmj->pij/dot_general | solution.py:28
  (1 shorter events, 0.0 us)
Async XLA Ops:
  6.5 8.1 %copy-start = (f32[1024,128]{1,0:T(8,128)S(1)}, f32[1024,128]{1,0:T(8,128)}, u32[]{:S(2)}) copy-start(f32[1024,128]{1,0:T(8,128)} %param.6) | copy-start | bytes 1572868
  6.5 0.9 %copy-start.2 = (f32[256,64]{0,1:T(8,128)S(1)}, f32[256,64]{0,1:T(8,128)}, u32[]{:S(2)}) copy-start(f32[256,64]{0,1:T(8,128)} %param.5) | copy-start | bytes 196612
  6.5 33.1 %all-gather.2.cloned.1.call-start = ((), (), s32[]{:S(2)}) async-start(), calls=%async_computation.1 | async-start | bytes 1310720 | tf_op jit(solution)/shard_map/all_gather | solution.py:13
  7.3 62.8 %reduce-scatter.2.cloned.1.call-start = ((), (), s32[]{:S(2)}) async-start(), calls=%async_computation.2 | async-start | bytes 1310720 | tf_op jit(solution)/shard_map/reduce_scatter | solution.py:17
  45.5 0.8 copy-start.1
Sparse Core Ops, SparseCore 0:
  8.9 30.6 all-gather.1
  45.7 24.3 reduce-scatter.1
where the time goes:
time: 88.4 us; the launch traced here: 88.1 us
  waiting for transfers between devices  49 us (55%)
  blocking collectives  15.9 us (18%)
  between operations  13.4 us (15%)
  matrix products  7.2 us (8%)
  local copies, waits for them, and re-layouts  2.45 us (3%)
    all_gather x1, waiting for transfers between devices, local(): whole = lax.all_gather(amplitudes, 'out', axis=2, tiled=True)  24.5 us
    reduce_scatter x1, waiting for transfers between devices, local(): lax.psum_scatter(product.reshape(lax.axis_size('con') * kept_rows, whole....  23.8 us
    all_gather x1, blocking collectives, local(): complete = lax.all_gather(right, 'occ', axis=1, tiled=True)  8.73 us
    all_gather x1, blocking collectives, local(): lax.all_gather(fit_out, 'con', axis=0, tiled=True)  7.21 us
    dot_general x1, matrix products, local(): product = jnp.dot(tile, flat, precision=highest)  4.32 us
  transfers between devices with their start and end apart: 2, of which 2 were waited for; matrix products, arithmetic and copies ran while one was open for 1% of the time, Pallas kernels for 0%

commit v1 on v0

v1 whole, which is shorter than its diff:
```python
import functools

import jax
import jax.numpy as jnp
from jax import lax
from jax.experimental import pallas as pl
from jax.experimental.pallas import tpu as pltpu
from jax.sharding import PartitionSpec as P

highest = lax.Precision.HIGHEST
MESH = pl.DeviceIdType.MESH
LANES = 128
VMEM_BYTES = 40 * 2**20


def split(a):
    hi = a.astype(jnp.bfloat16)
    lo = (a - hi.astype(jnp.float32)).astype(jnp.bfloat16)
    return hi, lo


def product(a, b_hi, b_lo, transposed=False):
    dims = (((1,), (1 if transposed else 0,)), ((), ()))
    dot = functools.partial(lax.dot_general, dimension_numbers=dims, preferred_element_type=jnp.float32)
    hi, lo = split(a)
    rows = a.shape[0]
    both = dot(jnp.concatenate([hi, lo], axis=0), b_hi)
    return both[:rows] + both[rows:] + dot(hi, b_lo)


def flip(index, bits):
    step = 1
    result = index
    while step <= bits:
        if bits & step:
            result = result + step * (1 - 2 * ((index // step) % 2))
        step *= 2
    return result


def kernel(
    sizes, amp_in, out_in, con_in, hole_in, result,
    amps, fit_out, fit_con, hole, dressed, mixer_hi, mixer_lo, tiles, partial, received, summed, last, pieces,
    local_sem, amp_sems, fit_sems, tile_sems, sum_sems, piece_sems,
):
    n_out, n_con, n_occ, own_i, own_n, naux_block, rows = sizes
    rounds = n_con.bit_length() - 1
    lanes = own_i * own_n
    norbs = own_i * n_occ
    group = LANES // own_n
    groups = own_i // group
    z, c, x = lax.axis_index("out"), lax.axis_index("con"), lax.axis_index("occ")

    loads = [
        pltpu.make_async_copy(hole_in, hole, local_sem.at[0]),
        pltpu.make_async_copy(out_in, fit_out.at[c], local_sem.at[1]),
        pltpu.make_async_copy(con_in, fit_con, local_sem.at[2]),
        pltpu.make_async_copy(amp_in, amps.at[x], local_sem.at[3]),
    ]
    for load in loads:
        load.start()

    z_peers = [flip(z, d) for d in range(n_out)]
    c_peers = [flip(c, d) for d in range(n_con)]
    x_peers = [flip(x, d) for d in range(n_occ)]
    barrier = pltpu.get_barrier_semaphore()
    for axis, peers in (("out", z_peers), ("con", c_peers), ("occ", x_peers)):
        for peer in peers[1:]:
            pl.semaphore_signal(barrier, inc=1, device_id={axis: peer}, device_id_type=MESH)
    pl.semaphore_wait(barrier, n_out + n_con + n_occ - 3)

    def send(src, dst, sems, slot, axis, peer):
        copy = pltpu.make_async_remote_copy(
            src_ref=src, dst_ref=dst, send_sem=sems.at[0, slot], recv_sem=sems.at[1, slot],
            device_id={axis: peer}, device_id_type=MESH,
        )
        copy.start()
        return copy

    fit_copies = {
        d: send(out_in, fit_out.at[c], fit_sems, d, "con", c_peers[d]) for d in reversed(range(1, n_con))
    }
    amp_copies = {d: send(amp_in, amps.at[x], amp_sems, d, "occ", x_peers[d]) for d in range(1, n_occ)}

    loads[0].wait()
    eye = (
        lax.broadcasted_iota(jnp.int32, (norbs, norbs), 0) == lax.broadcasted_iota(jnp.int32, (norbs, norbs), 1)
    ).astype(jnp.float32)
    dress = eye - hole[...]
    repeats = LANES // norbs
    turned = jnp.transpose(jnp.concatenate([dress] * repeats, axis=0))
    row_group = lax.broadcasted_iota(jnp.int32, (LANES, LANES), 0) // own_n
    lane_group = lax.broadcasted_iota(jnp.int32, (LANES, LANES), 1) // norbs
    for o in range(n_out):
        block = jnp.concatenate([turned[o * own_n : (o + 1) * own_n]] * group, axis=0)
        for t in range(group // repeats):
            hi, lo = split(jnp.where(row_group == lane_group + t * repeats, block, 0.0))
            at = (slice(o * LANES, (o + 1) * LANES), slice(t * LANES, (t + 1) * LANES))
            mixer_hi[at] = hi
            mixer_lo[at] = lo

    loads[1].wait()
    loads[2].wait()
    tile = None
    for d in range(n_con):
        if d > 0:
            fit_copies[d].wait_recv()
        owner = c_peers[d]
        con_hi, con_lo = split(fit_con[pl.ds(pl.multiple_of(owner * naux_block, naux_block), naux_block), :])
        term = product(fit_out[owner], con_hi, con_lo)
        tile = term if tile is None else tile + term
    tiles[z] = tile
    tile_copies = {
        d: send(tiles.at[z], tiles.at[z], tile_sems, d, "out", z_peers[d]) for d in reversed(range(1, n_out))
    }

    first = pl.multiple_of(x * own_i, own_i)
    own_rows = lax.broadcasted_iota(jnp.int32, (own_i, norbs), 0) + first
    own_eye = (own_rows == lax.broadcasted_iota(jnp.int32, (own_i, norbs), 1)).astype(jnp.float32)
    own_dress = own_eye - hole[pl.ds(first, own_i), :]
    loads[3].wait()
    for d in range(1, n_occ):
        amp_copies[d].wait_recv()
    wide = dressed.shape[1]
    for n in range(0, own_n, 2):
        parts = [
            jnp.concatenate([amps[o, pl.ds(m, own_i, stride=own_n), :] for o in range(n_occ)], axis=0)
            for m in (n, n + 1)
        ]
        hi, lo = split(jnp.concatenate(parts, axis=1))
        value = product(own_dress, hi, lo)
        dressed[pl.ds(n, own_i, stride=own_n), :] = value[:, :wide]
        dressed[pl.ds(n + 1, own_i, stride=own_n), :] = value[:, wide:]
    amp_hi, amp_lo = split(dressed[...])

    sum_copies = {}
    half = n_con // 2
    for d in range(n_out):
        o = z_peers[d]
        if d > 0:
            tile_copies[d].wait_recv()
        value = product(tiles[o], amp_hi, amp_lo, transposed=True)
        partial[o] = value.reshape(half, 2, rows, lanes)
        sum_copies[0, d] = send(
            partial.at[o, :, 1 - c % 2], received.at[o, pl.ds(0, half)], sum_sems, d, "con", c_peers[1]
        )
    piece_copies = {}
    base = 0
    for r in range(rounds):
        count = n_con >> (r + 1)
        for d in range(n_out):
            o = z_peers[d]
            sum_copies[r, d].wait_recv()
            if r == 0:
                total = partial[o, :, c % 2] + received[o, :count]
            else:
                total = summed[o, pl.ds(before + (c // 2**r) % 2, count)] + received[o, base : base + count]
            if r < rounds - 1:
                summed[o, base : base + count] = total
                bit = (c // 2 ** (r + 1)) % 2
                sum_copies[r + 1, d] = send(
                    summed.at[o, pl.ds(base + 1 - bit, count // 2)],
                    received.at[o, pl.ds(base + count, count // 2)],
                    sum_sems, (r + 1) * n_out + d, "con", c_peers[2 ** (r + 1)],
                )
            elif d == 0:
                pieces[o] = total[0]
            else:
                last[o] = total[0]
                piece_copies[d] = send(last.at[o], pieces.at[z], piece_sems, d, "out", o)
        before = base
        base += count

    for d in range(1, n_out):
        piece_copies[d].wait_recv()
    columns = [
        jnp.concatenate([pieces[o, :, g * LANES : (g + 1) * LANES] for g in range(groups)], axis=0)
        for o in range(n_out)
    ]
    final = product(jnp.concatenate(columns, axis=1), mixer_hi[...], mixer_lo[...])
    for t in range(group // repeats):
        lane_tile = final[:, t * LANES : (t + 1) * LANES]
        for s in range(repeats):
            turn = lane_tile if s == 0 else pltpu.roll(lane_tile, LANES - s * norbs, axis=1)
            for g in range(groups):
                i = g * group + t * repeats + s
                result[pl.ds(i, rows, stride=own_i), :] = turn[g * rows : (g + 1) * rows]

    for copies in (fit_copies, amp_copies, tile_copies, sum_copies, piece_copies):
        for copy in copies.values():
            copy.wait_send()


def fused(n_out, n_con, n_occ, amplitudes, fit_out, fit_con, hole_hole):
    pairs, own_i, own_n = amplitudes.shape
    naux_block, own_out = fit_out.shape
    naux = fit_con.shape[0]
    norbs = hole_hole.shape[0]
    rows = own_out // n_con
    lanes = own_i * own_n
    rounds = n_con.bit_length() - 1
    f32, bf16 = jnp.float32, jnp.bfloat16
    wide = (LANES // own_n) * norbs
    dma = pltpu.SemaphoreType.DMA
    result = pl.pallas_call(
        functools.partial(kernel, (n_out, n_con, n_occ, own_i, own_n, naux_block, rows)),
        out_shape=jax.ShapeDtypeStruct((rows * own_i, LANES), f32),
        in_specs=[pl.BlockSpec(memory_space=pl.ANY)] * 4,
        out_specs=pl.BlockSpec(memory_space=pltpu.VMEM),
        scratch_shapes=[
            pltpu.VMEM((n_occ, lanes, pairs), f32),
            pltpu.VMEM((n_con, own_out, naux_block), f32),
            pltpu.VMEM((naux, pairs), f32),
            pltpu.VMEM((norbs, norbs), f32),
            pltpu.VMEM((lanes, pairs), f32),
            pltpu.VMEM((n_out * LANES, wide), bf16),
            pltpu.VMEM((n_out * LANES, wide), bf16),
            pltpu.VMEM((n_out, own_out, pairs), f32),
            pltpu.VMEM((n_out, n_con // 2, 2, rows, lanes), f32),
            pltpu.VMEM((n_out, n_con - 1, rows, lanes), f32),
            pltpu.VMEM((n_out, n_con - 1, rows, lanes), f32),
            pltpu.VMEM((n_out, rows, lanes), f32),
            pltpu.VMEM((n_out, rows, lanes), f32),
            dma((4,)),
            dma((2, n_occ)),
            dma((2, n_con)),
            dma((2, n_out)),
            dma((2, n_out * rounds)),
            dma((2, n_out)),
        ],
        compiler_params=pltpu.CompilerParams(
            collective_id=0, has_side_effects=True, vmem_limit_bytes=VMEM_BYTES
        ),
    )(
        amplitudes.transpose(1, 2, 0).reshape(lanes, pairs),
        fit_out.T,
        fit_con,
        hole_hole,
    )
    return result[:, :norbs].reshape(rows, own_i, norbs)


def unfused(amplitudes, fit_out, fit_con, hole_hole):
    norbs = hole_hole.shape[0]
    dress = jnp.eye(norbs, dtype=jnp.float32) - hole_hole
    tile = jnp.dot(lax.all_gather(fit_out, "con", axis=0, tiled=True).T, fit_con, precision=highest)
    whole = lax.all_gather(amplitudes, "out", axis=2, tiled=True)
    kept_rows = tile.shape[0] // lax.axis_size("con")
    flat = whole.reshape(whole.shape[0], -1)
    total = jnp.dot(tile, flat, precision=highest)
    summed = lax.psum_scatter(
        total.reshape(lax.axis_size("con") * kept_rows, whole.shape[1], whole.shape[2]),
        "con",
        scatter_dimension=0,
        tiled=True,
    )
    right = jnp.einsum("qim,jm->qij", summed, dress, precision=highest)
    complete = lax.all_gather(right, "occ", axis=1, tiled=True)
    own = summed.shape[1]
    first = lax.axis_index("occ") * own
    rows_dress = lax.dynamic_slice_in_dim(dress, first, own, 0)
    return jnp.einsum("im,pmj->pij", rows_dress, complete, precision=highest)


def fits(n_out, n_con, n_occ, amplitudes, fit_out, fit_con, hole_hole):
    pairs, own_i, own_n = amplitudes.shape
    naux_block, own_out = fit_out.shape
    norbs = hole_hole.shape[0]
    lanes = own_i * own_n
    powers = all(n > 1 and n & (n - 1) == 0 for n in (n_out, n_con, n_occ))
    if not powers or own_out % n_con or LANES % own_n or LANES % norbs or own_n % 8 or pairs != LANES:
        return False
    if own_i % (LANES // own_n) or (LANES // own_n) % (LANES // norbs) or own_i % 8:
        return False
    if (own_out // n_con) % 8 or naux_block % LANES or n_con > 4:
        return False
    words = n_out * lanes * (own_out // n_con) * (3 * n_con) + fit_con.size * (3 + n_con * own_out // pairs)
    return 4 * words < VMEM_BYTES // 2


def solution(mesh):
    counts = mesh.shape["out"], mesh.shape["con"], mesh.shape["occ"]

    def local(*arrays):
        if fits(*counts, *arrays):
            return fused(*counts, *arrays)
        return unfused(*arrays)

    placed = (P("con", "occ", "out"), P("con", "out"), P(None, "con"), P())
    return jax.shard_map(
        local, mesh=mesh, in_specs=placed, out_specs=P(("out", "con"), "occ", None), check_vma=False
    )
```

time: 88.4 us -> 28.8 us (0.33)
  waiting for transfers between devices: 49 us -> 0 us
  Pallas kernels: 0 us -> 24.2 us
  blocking collectives: 15.9 us -> 0 us
  between operations: 13.4 us -> 0.01 us
  matrix products: 7.2 us -> 0 us
  local copies, waits for them, and re-layouts: 2.45 us -> 4.29 us
    all_gather x1 -> x0, waiting for transfers between devices: 24.5 us -> none  [local(): whole = lax.all_gather(amplitudes, 'out', axis=2, tiled=True)]
    pallas_call x0 -> x1, Pallas kernels: none -> 24.2 us  [fused(): pl.pallas_call(functools.partial(kernel, (n_out, n_con, n_occ, own_i, own...]
    reduce_scatter x1 -> x0, waiting for transfers between devices: 23.8 us -> none  [local(): lax.psum_scatter(product.reshape(lax.axis_size('con') * kept_rows, whole....]
    all_gather x2 -> x0, blocking collectives: 15.9 us -> none  [the longest x1 8.73 us: local(): complete = lax.all_gather(right, 'occ', axis=1, tiled=True)]
    dot_general x4 -> x0, matrix products: 7.2 us -> none  [the longest x1 4.32 us: local(): product = jnp.dot(tile, flat, precision=highest)]
    unnamed x6 -> x9, local copies, waits for them, and re-layouts: 0.86 us -> 4.29 us
    dot_general x1 -> x0, local copies, waits for them, and re-layouts: 1.59 us -> none  [local(): product = jnp.dot(tile, flat, precision=highest)]
  transfers between devices with their start and end apart: 2 -> 0, of which waited for: 2 -> 0; matrix products, arithmetic and copies ran while one was open for 1% -> 0% of each run, Pallas kernels for 0% -> 0%
where the time goes in v1:
time: 28.8 us; the launch traced here: 28.5 us
  Pallas kernels  24.2 us (84%)
  local copies, waits for them, and re-layouts  4.29 us (15%)
    pallas_call x1, Pallas kernels, fused(): pl.pallas_call(functools.partial(kernel, (n_out, n_con, n_occ, own_i, own...  24.2 us
    unnamed x9, local copies, waits for them, and re-layouts  4.29 us

profile of v1, /device:TPU:0, one launch (start us, length us, event | category | flops | bytes accessed | tf_op | source)
XLA Modules:
  0.0 28.5 jit_solution(16448729540090835779)
XLA Ops:
  0.0 0.0 copy-start
  0.0 1.0 %copy-done = f32[1024,128]{1,0:T(8,128)S(1)} copy-done((f32[1024,128]{1,0:T(8,128)S(1)}, f32[1024,128]{1,0:T(8,128)}, u32[]{:S(2)}) %copy-start) | copy-done | bytes 524312
  1.0 0.0 copy-start.1
  1.0 0.9 %copy-done.1 = f32[128,32,16]{0,2,1:T(8,128)S(1)} copy-done((f32[128,32,16]{0,2,1:T(8,128)S(1)}, f32[128,32,16]{0,2,1:T(8,128)}, u32[]{:S(2)}) %copy-start.1) | copy-done | bytes 262168
  2.0 0.0 copy-start.2
  2.0 0.8 %copy-done.2 = f32[256,64]{0,1:T(8,128)S(1)} copy-done((f32[256,64]{0,1:T(8,128)S(1)}, f32[256,64]{0,1:T(8,128)}, u32[]{:S(2)}) %copy-start.2) | copy-done | bytes 65560
  2.8 0.0 copy-start.3
  2.8 0.8 %copy-done.3 = f32[64,64]{1,0:T(8,128)S(1)} copy-done((f32[64,64]{1,0:T(8,128)S(1)}, f32[64,64]{1,0:T(8,128)}, u32[]{:S(2)}) %copy-start.3) | copy-done | bytes 16408
  3.6 24.2 %shard_map.46 = f32[512,128]{1,0:T(8,128)S(1)} custom-call(f32[512,128]{1,0:T(8,128)S(1)} %bitcast.7, f32[64,256]{1,0:T(8,128)S(1)} %bitcast.8, f32[1024,128]{1,0:T(8,128)S(1)} %copy-done, f32[64,64]{1,0:T(8,128)S(1)} %copy-done.3), custom_call_target="tpu_custom_call" | custom-call | tf_op jit(solution)/shard_map/pallas_call | solution.py:205
  27.8 0.7 %copy.6 = f32[16,32,64]{2,1,0:T(8,128)} copy(f32[16,32,64]{2,1,0:T(8,128)S(1)} %bitcast.6) | data formatting | bytes 262144
Async XLA Ops:
  0.0 1.0 %copy-start = (f32[1024,128]{1,0:T(8,128)S(1)}, f32[1024,128]{1,0:T(8,128)}, u32[]{:S(2)}) copy-start(f32[1024,128]{1,0:T(8,128)} %con_in.1) | copy-start | bytes 1572868
  1.0 0.9 %copy-start.1 = (f32[128,32,16]{0,2,1:T(8,128)S(1)}, f32[128,32,16]{0,2,1:T(8,128)}, u32[]{:S(2)}) copy-start(f32[128,32,16]{0,2,1:T(8,128)} %param.4) | copy-start | bytes 786436
  2.0 0.8 %copy-start.2 = (f32[256,64]{0,1:T(8,128)S(1)}, f32[256,64]{0,1:T(8,128)}, u32[]{:S(2)}) copy-start(f32[256,64]{0,1:T(8,128)} %param.5) | copy-start | bytes 196612
  2.8 0.8 %copy-start.3 = (f32[64,64]{1,0:T(8,128)S(1)}, f32[64,64]{1,0:T(8,128)}, u32[]{:S(2)}) copy-start(f32[64,64]{1,0:T(8,128)} %hole_in.1) | copy-start | bytes 49156

commit v2 on v1

--- a/solution.py
+++ b/solution.py
@@ -10,7 +10,7 @@
 highest = lax.Precision.HIGHEST
 MESH = pl.DeviceIdType.MESH
 LANES = 128
-VMEM_BYTES = 40 * 2**20
+VMEM_BYTES = 60 * 2**20
 
 
 def split(a):

time: 28.8 us -> 26.7 us (0.927)
  local copies, waits for them, and re-layouts: 4.29 us -> 1.67 us
  Pallas kernels: 24.2 us -> 24.9 us
    unnamed x9 -> x1, local copies, waits for them, and re-layouts: 4.29 us -> 1.67 us
    pallas_call x1, Pallas kernels: 24.2 us -> 24.9 us  [fused(): pl.pallas_call(functools.partial(kernel, (n_out, n_con, n_occ, own_i, own...]
where the time goes in v2:
time: 26.7 us; the launch traced here: 26.5 us
  Pallas kernels  24.9 us (93%)
  local copies, waits for them, and re-layouts  1.67 us (6%)
    pallas_call x1, Pallas kernels, fused(): pl.pallas_call(functools.partial(kernel, (n_out, n_con, n_occ, own_i, own...  24.9 us
    unnamed x1, local copies, waits for them, and re-layouts  1.67 us

profile of v2, /device:TPU:0, one launch (start us, length us, event | category | flops | bytes accessed | tf_op | source)
XLA Modules:
  0.0 26.5 jit_solution(11915125649388237077)
XLA Ops:
  0.0 24.9 %shard_map.46 = f32[512,128]{1,0:T(8,128)} custom-call(f32[512,128]{1,0:T(8,128)} %bitcast.7, f32[64,256]{1,0:T(8,128)} %bitcast.8, f32[1024,128]{1,0:T(8,128)} %con_in.1, f32[64,64]{1,0:T(8,128)} %hole_in.1), custom_call_target="tpu_custom_call" | custom-call | tf_op jit(solution)/shard_map/pallas_call | solution.py:205
  24.9 1.7 %copy.6 = f32[16,32,64]{2,1,0:T(8,128)} copy(f32[16,32,64]{2,1,0:T(8,128)} %bitcast.6) | data formatting | bytes 262144

commit v3 on v2

--- a/solution.py
+++ b/solution.py
@@ -41,7 +41,7 @@
 def kernel(
     sizes, amp_in, out_in, con_in, hole_in, result,
     amps, fit_out, fit_con, hole, dressed, mixer_hi, mixer_lo, tiles, partial, received, summed, last, pieces,
-    local_sem, amp_sems, fit_sems, tile_sems, sum_sems, piece_sems,
+    local_sem, amp_sems, fit_sems, tile_sems, sum_sems, piece_sems, news,
 ):
     n_out, n_con, n_occ, own_i, own_n, naux_block, rows = sizes
     rounds = n_con.bit_length() - 1
@@ -64,10 +64,35 @@
     c_peers = [flip(c, d) for d in range(n_con)]
     x_peers = [flip(x, d) for d in range(n_occ)]
     barrier = pltpu.get_barrier_semaphore()
-    for axis, peers in (("out", z_peers), ("con", c_peers), ("occ", x_peers)):
+    for axis, peers in (("con", c_peers), ("occ", x_peers)):
         for peer in peers[1:]:
             pl.semaphore_signal(barrier, inc=1, device_id={axis: peer}, device_id_type=MESH)
-    pl.semaphore_wait(barrier, n_out + n_con + n_occ - 3)
+    for ahead in (1, -1):
+
+        @pl.when((z + ahead >= 0) & (z + ahead < n_out))
+        def _():
+            pl.semaphore_signal(barrier, inc=1, device_id={"out": z + ahead}, device_id_type=MESH)
+
+    neighbours = jnp.minimum(z, 1) + jnp.minimum(n_out - 1 - z, 1)
+    pl.semaphore_wait(barrier, n_con + n_occ - 2 + neighbours)
+
+    def tell(k):
+        for ahead in (1, -1):
+            about = z - ahead * (k - 1)
+
+            @pl.when((z + ahead >= 0) & (z + ahead < n_out) & (about >= 0) & (about < n_out))
+            def _():
+                pl.semaphore_signal(
+                    news.at[(1 + ahead) // 2, k], inc=1, device_id={"out": z + ahead}, device_id_type=MESH
+                )
+
+    def hear(k):
+        for ahead in (1, -1):
+            about = z - ahead * k
+
+            @pl.when((about >= 0) & (about < n_out))
+            def _():
+                pl.semaphore_wait(news.at[(1 + ahead) // 2, k], 1)
 
     def send(src, dst, sems, slot, axis, peer):
         copy = pltpu.make_async_remote_copy(
@@ -81,6 +106,9 @@
         d: send(out_in, fit_out.at[c], fit_sems, d, "con", c_peers[d]) for d in reversed(range(1, n_con))
     }
     amp_copies = {d: send(amp_in, amps.at[x], amp_sems, d, "occ", x_peers[d]) for d in range(1, n_occ)}
+
+    if n_out > 2:
+        tell(2)
 
     loads[0].wait()
     eye = (
@@ -98,6 +126,11 @@
             at = (slice(o * LANES, (o + 1) * LANES), slice(t * LANES, (t + 1) * LANES))
             mixer_hi[at] = hi
             mixer_lo[at] = lo
+
+    for k in range(2, n_out):
+        hear(k)
+        if k + 1 < n_out:
+            tell(k + 1)
 
     loads[1].wait()
     loads[2].wait()
@@ -133,9 +166,10 @@
         dressed[pl.ds(n + 1, own_i, stride=own_n), :] = value[:, wide:]
     amp_hi, amp_lo = split(dressed[...])
 
-    sum_copies = {}
+    sum_copies, piece_copies = {}, {}
     half = n_con // 2
-    for d in range(n_out):
+
+    def multiply(d):
         o = z_peers[d]
         if d > 0:
             tile_copies[d].wait_recv()
@@ -144,32 +178,40 @@
         sum_copies[0, d] = send(
             partial.at[o, :, 1 - c % 2], received.at[o, pl.ds(0, half)], sum_sems, d, "con", c_peers[1]
         )
-    piece_copies = {}
-    base = 0
-    for r in range(rounds):
+
+    def fold(r, d):
+        o = z_peers[d]
         count = n_con >> (r + 1)
-        for d in range(n_out):
-            o = z_peers[d]
-            sum_copies[r, d].wait_recv()
-            if r == 0:
-                total = partial[o, :, c % 2] + received[o, :count]
-            else:
-                total = summed[o, pl.ds(before + (c // 2**r) % 2, count)] + received[o, base : base + count]
-            if r < rounds - 1:
-                summed[o, base : base + count] = total
-                bit = (c // 2 ** (r + 1)) % 2
-                sum_copies[r + 1, d] = send(
-                    summed.at[o, pl.ds(base + 1 - bit, count // 2)],
-                    received.at[o, pl.ds(base + count, count // 2)],
-                    sum_sems, (r + 1) * n_out + d, "con", c_peers[2 ** (r + 1)],
-                )
-            elif d == 0:
-                pieces[o] = total[0]
-            else:
-                last[o] = total[0]
-                piece_copies[d] = send(last.at[o], pieces.at[z], piece_sems, d, "out", o)
-        before = base
-        base += count
+        base = n_con - (n_con >> r)
+        sum_copies[r, d].wait_recv()
+        if r == 0:
+            total = partial[o, :, c % 2] + received[o, :count]
+        else:
+            before = n_con - (n_con >> (r - 1))
+            total = summed[o, pl.ds(before + (c // 2**r) % 2, count)] + received[o, base : base + count]
+        if r < rounds - 1:
+            summed[o, base : base + count] = total
+            bit = (c // 2 ** (r + 1)) % 2
+            sum_copies[r + 1, d] = send(
+                summed.at[o, pl.ds(base + 1 - bit, count // 2)],
+                received.at[o, pl.ds(base + count, count // 2)],
+                sum_sems, (r + 1) * n_out + d, "con", c_peers[2 ** (r + 1)],
+            )
+        elif d == 0:
+            pieces[o] = total[0]
+        else:
+            last[o] = total[0]
+            piece_copies[d] = send(last.at[o], pieces.at[z], piece_sems, d, "out", o)
+
+    order = tuple(reversed(range(n_out)))
+    for k, d in enumerate(order):
+        multiply(d)
+        if k > 0:
+            fold(0, order[k - 1])
+    fold(0, order[-1])
+    for r in range(1, rounds):
+        for d in reversed(range(n_out)):
+            fold(r, d)
 
     for d in range(1, n_out):
         piece_copies[d].wait_recv()
@@ -227,6 +269,7 @@
             dma((2, n_out)),
             dma((2, n_out * rounds)),
             dma((2, n_out)),
+            pltpu.SemaphoreType.REGULAR((2, n_out)),
         ],
         compiler_params=pltpu.CompilerParams(
             collective_id=0, has_side_effects=True, vmem_limit_bytes=VMEM_BYTES

time: 26.7 us -> 25.2 us (0.944)
  Pallas kernels: 24.9 us -> 23.4 us
    pallas_call x1, Pallas kernels: 24.9 us -> 23.4 us  [fused(): pl.pallas_call(functools.partial(kernel, (n_out, n_con, n_occ, own_i, own...]
where the time goes in v3:
time: 25.2 us; the launch traced here: 25.1 us
  Pallas kernels  23.4 us (93%)
  local copies, waits for them, and re-layouts  1.67 us (7%)
    pallas_call x1, Pallas kernels, fused(): pl.pallas_call(functools.partial(kernel, (n_out, n_con, n_occ, own_i, own...  23.4 us
    unnamed x1, local copies, waits for them, and re-layouts  1.67 us

profile of v3, /device:TPU:0, one launch (start us, length us, event | category | flops | bytes accessed | tf_op | source)
XLA Modules:
  0.0 25.1 jit_solution(4715673535305492704)
XLA Ops:
  0.0 23.4 %shard_map.46 = f32[512,128]{1,0:T(8,128)} custom-call(f32[512,128]{1,0:T(8,128)} %bitcast.7, f32[64,256]{1,0:T(8,128)} %bitcast.8, f32[1024,128]{1,0:T(8,128)} %con_in.1, f32[64,64]{1,0:T(8,128)} %hole_in.1), custom_call_target="tpu_custom_call" | custom-call | tf_op jit(solution)/shard_map/pallas_call | solution.py:247
  23.4 1.7 %copy.6 = f32[16,32,64]{2,1,0:T(8,128)} copy(f32[16,32,64]{2,1,0:T(8,128)} %bitcast.6) | data formatting | bytes 262144
